TPU v7x, 32 devices: a whole 2x2x4 slice. The times are simulated.
32 devices in a mesh: row: 2 (over y), col: 4 (over x, core), layer: 4 (over z).
Axes of the slice: x: 2, y: 2, z: 4, core: 2. Of those that a mesh axis runs over, the one named last changes fastest.
Arguments:
- a_vals: bfloat16 [48, 4, 8, 64, 128], P('row', 'layer', 'col'), may hold values from -0.375 to 0.375
- a_cols: int32 [48, 4, 8, 2], P('row', 'layer', 'col'), may hold values from 0 to 7, as said below
- a_count: int32 [48, 4, 8], P('row', 'layer', 'col'), may hold values from 0 to 2, as said below
- panel_map: int32 [4, 8], replicated, may hold values from 0 to 7, each once within a row
- p_vals: bfloat16 [4, 8, 8, 4, 64, 256], P('layer', 'row', None, 'col'), may hold values from -6 to 6
- p_cols: int32 [4, 8, 8, 4, 4], P('layer', 'row', None, 'col'), may hold values from 0 to 7, as said below
- p_count: int32 [4, 8, 8, 4], P('layer', 'row', None, 'col'), may hold values from 0 to 4, as said below
Outputs:
- product: bfloat16 [3072, 2048], P(('row', 'col', 'layer'))
Inputs may be any that keep to these rules, and one draw needn't show every extreme that they name: `a_count`: each block row has at most 27 valid operator blocks in all, some block row exactly 27, and some entry reaches 2. `a_cols`: the slots of one block row and section name distinct block columns. `p_cols`: the slots of one block row and group name distinct coarse columns. `p_count`: reaches 4 somewhere in every draw.
All inputs are finite; a program needn't handle non-finite values.
Results may differ from a plain program's by a relative error of at most 0.001.
Values may be sent and summed in bfloat16 or wider, within the bound.
A program may use at most 128 MiB of HBM per device.

v0:
```python
import jax
import jax.numpy as jnp
from jax import lax
from jax.sharding import PartitionSpec as P

CB = 8


def expand(blocks, cols, count):
    panel_rows, groups, block_side, wide = blocks.shape
    slot_count = cols.shape[2]
    pieces_view = blocks.reshape(panel_rows, groups, block_side, slot_count, block_side)
    valid_mask = jnp.arange(slot_count)[None, None, :] < count[:, :, None]
    onehot = (
        (cols[:, :, :, None] == jnp.arange(CB)[None, None, None, :]) & valid_mask[:, :, :, None]
    ).astype(jnp.bfloat16)
    dense_rows = jnp.einsum(
        "kgytz,kgtc->kygcz", pieces_view, onehot, preferred_element_type=jnp.float32
    )
    return dense_rows.astype(jnp.bfloat16).reshape(panel_rows, block_side, groups * CB * block_side)


def accumulate(running, a_panel, a_cols_panel, a_count_panel, dense_rows):
    rows_blk, block_side, wide = a_panel.shape
    slot_count = a_cols_panel.shape[1]
    valid_mask = (jnp.arange(slot_count)[None, :] < a_count_panel[:, None]).astype(jnp.bfloat16)
    masked = (
        a_panel.reshape(rows_blk, block_side, slot_count, block_side) * valid_mask[:, None, :, None]
    ).reshape(rows_blk, block_side, wide)
    picked = jnp.take(dense_rows, a_cols_panel, axis=0).reshape(
        rows_blk, slot_count * block_side, dense_rows.shape[2]
    )
    return running + jnp.einsum("ixk,ikn->ixn", masked, picked, preferred_element_type=jnp.float32)


def pick_panel(array, panel_idx):
    return lax.dynamic_index_in_dim(array, panel_idx, 0, keepdims=False)


def body(a_vals, a_cols, a_count, panel_map, p_vals, p_cols, p_count):
    rows_blk = a_vals.shape[0]
    block_side = a_vals.shape[3]
    held_sections = a_vals.shape[2]
    layer_map = lax.dynamic_index_in_dim(panel_map, lax.axis_index("layer"), 0, keepdims=False)
    section_vals, section_cols, section_count = (
        lax.all_gather(p_vals, "row", axis=1, tiled=True),
        lax.all_gather(p_cols, "row", axis=1, tiled=True),
        lax.all_gather(p_count, "row", axis=1, tiled=True),
    )
    full_vals, full_cols, full_count = (
        lax.all_gather(section_vals, "col", axis=3, tiled=True),
        lax.all_gather(section_cols, "col", axis=3, tiled=True),
        lax.all_gather(section_count, "col", axis=3, tiled=True),
    )
    width_all = full_vals.shape[3] * CB * block_side
    running = jnp.zeros((rows_blk, block_side, width_all), jnp.float32)
    first_section = lax.axis_index("col") * held_sections
    for section_slot in range(held_sections):
        panel_idx = pick_panel(layer_map, first_section + section_slot)
        dense_rows = expand(
            pick_panel(full_vals[0], panel_idx),
            pick_panel(full_cols[0], panel_idx),
            pick_panel(full_count[0], panel_idx),
        )
        running = accumulate(
            running,
            a_vals[:, 0, section_slot],
            a_cols[:, 0, section_slot],
            a_count[:, 0, section_slot],
            dense_rows,
        )
    partial_terms = running.reshape(rows_blk * block_side, width_all)
    return lax.psum_scatter(
        partial_terms, ("col", "layer"), scatter_dimension=0, tiled=True
    ).astype(jnp.bfloat16)


def solution(mesh):
    placed = (
        P("row", "layer", "col", None, None),
        P("row", "layer", "col", None),
        P("row", "layer", "col"),
        P(),
        P("layer", "row", None, "col", None, None),
        P("layer", "row", None, "col", None),
        P("layer", "row", None, "col"),
    )
    return jax.shard_map(
        body,
        mesh=mesh,
        in_specs=placed,
        out_specs=P(("row", "col", "layer"), None),
        check_vma=False,
    )
```

profile of v0, /device:TPU:7, one launch (start us, length us, event | category | flops | bytes accessed | tf_op | source)
XLA Modules:
  0.0 327.5 jit_solution(12131205655907332897)
XLA Ops:
  6.5 0.7 all-gather.3.cloned.1.call-update
  7.3 0.0 all-gather.5.cloned.1.call-start
  7.3 35.0 %all-gather.3.cloned.1.call-done = bf16[1,8,8,1,64,256]{5,4,3,2,0,1:T(8,128)(2,1)} async-done(((bf16[1,4,8,1,64,256]{5,4,3,2,0,1:T(8,128)(2,1)}), bf16[1,8,8,1,64,256]{5,4,3,2,0,1:T(8,128)(2,1)}) %all-gather.3.cloned.1.call-update) | async-done | bytes 2097168 | tf_op jit(solution)/shard_map/all_gather | solution.py:46
  42.3 0.0 all-gather.5.cloned.1.call-update
  42.3 0.0 reduce-scatter.2.cloned.1.call-start
  42.4 1.4 fusion.17
  46.5 0.7 compare_and_fusion
  47.2 0.1 copy.35
  47.3 0.1 copy.26
  47.4 0.7 compare_select_fusion
  48.1 0.1 copy.39
  48.2 0.1 reshape.143
  48.3 0.8 slice_bitcast_fusion
  49.0 0.1 fusion.15
  49.1 0.1 mul.29
  49.2 0.1 mul.30
  49.3 0.1 mul.34
  49.4 0.1 mul.35
  50.8 3.3 %all_gather.20 = s32[1,8,8,1]{2,3,0,1:T(1,128)S(1)} all-gather(s32[1,4,8,1]{2,3,0,1:T(1,128)} %bitcast.75), channel_id=1, replica_groups=mesh['row'=2,'col'=4,'layer'=4] {'row'}, dimensions={1}, use_global_device_ids=true | all-gather | bytes 384 | tf_op jit(solution)/shard_map/all_gather | solution.py:48
  54.2 6.8 %all_gather.21 = s32[1,8,8,4]{2,1,0,3:T(8,128)S(1)} all-gather(s32[1,8,8,1]{2,1,0,3:T(8,128)S(1)} %bitcast.71), channel_id=1, replica_groups=mesh['row'=2,'col'=4,'layer'=4] {'col'}, dimensions={3}, use_global_device_ids=true | all-gather | bytes 1280 | tf_op jit(solution)/shard_map/all_gather | solution.py:53
  61.0 0.1 copy.31
  61.1 0.1 copy.37
  61.2 0.1 copy.34
  61.2 0.1 reshape.139
  61.3 3.8 %all_gather.18 = s32[1,8,8,1,4]{2,4,3,0,1:T(4,128)S(1)} all-gather(s32[1,4,8,1,4]{2,4,3,0,1:T(4,128)} %bitcast.72), channel_id=1, replica_groups=mesh['row'=2,'col'=4,'layer'=4] {'row'}, dimensions={1}, use_global_device_ids=true | all-gather | bytes 1536 | tf_op jit(solution)/shard_map/all_gather | solution.py:47
  65.1 6.3 %all_gather.19 = s32[1,8,8,4,4]{2,4,3,0,1:T(4,128)S(1)} all-gather(s32[1,8,8,1,4]{2,4,3,0,1:T(4,128)S(1)} %all_gather.18), channel_id=1, replica_groups=mesh['row'=2,'col'=4,'layer'=4] {'col'}, dimensions={3}, use_global_device_ids=true | all-gather | bytes 5120 | tf_op jit(solution)/shard_map/all_gather | solution.py:52
  71.5 0.1 copy.36
  71.6 0.1 copy.28
  71.7 0.1 iota_compare_fusion.3
  71.8 0.1 iota_compare_fusion.2
  71.9 31.2 %all-gather.5.cloned.1.call-done = bf16[1,8,8,4,64,256]{5,4,3,2,0,1:T(8,128)(2,1)} async-done(((bf16[1,8,8,1,64,256]{5,4,3,2,0,1:T(8,128)(2,1)}), bf16[1,8,8,4,64,256]{5,4,3,2,0,1:T(8,128)(2,1)}) %all-gather.5.cloned.1.call-update) | async-done | bytes 8388624 | tf_op jit(solution)/shard_map/all_gather | solution.py:51
  103.1 2.8 constant_dynamic-slice_fusion
  105.9 3.3 %reshape.115 = bf16[8,4,64,4,64]{4,3,2,1,0:T(4,128)(2,1)S(1)} reshape(bf16[1,1,8,4,64,256]{5,4,3,2,0,1:T(8,128)(2,1)} %get-tuple-element.6) | data formatting | bytes 2097152 | tf_op jit(solution)/shard_map/reshape | solution.py:12
  109.2 1.9 convert_bitcast_fusion
  111.1 2.7 copy.38
  113.8 5.8 %reshape.116 = bf16[8,64,2048]{2,1,0:T(8,128)(2,1)S(1)} reshape(bf16[8,64,4,8,64]{4,3,2,1,0:T(8,128)(2,1)} %copy.38) | data formatting | bytes 4194304 | tf_op jit(solution)/shard_map/reshape | solution.py:20
  119.6 1.8 reshape.112
  121.4 3.1 convert_bitcast_fusion.1
  124.6 2.7 copy.33
  127.3 6.8 %reshape.113 = bf16[8,64,2048]{2,1,0:T(8,128)(2,1)} reshape(bf16[8,64,4,8,64]{4,3,2,1,0:T(8,128)(2,1)} %copy.33) | data formatting | bytes 4194304 | tf_op jit(solution)/shard_map/reshape | solution.py:20
  134.1 7.8 %gather_fusion = bf16[48,64,2048]{2,1,0:T(8,128)(2,1)} fusion(bf16[8,64,2048]{2,1,0:T(8,128)(2,1)} %reshape.113, s32[1024]{0:T(1024)S(1)} %pad_clamp_fusion.1), kind=kCustom, calls=%fused_computation.clone | custom fusion | bytes 25166016 | tf_op jit(solution)/shard_map/jit(_take)/gather | solution.py:30
  141.9 10.7 %broadcast_select_fusion.1 = bf16[24,2,64,2048]{3,2,1,0:T(8,128)(2,1)} fusion(bf16[24,2,64,2048]{3,2,1,0:T(8,128)(2,1)} %bitcast.68, pred[24,2]{1,0:T(8,128)(4,1)S(1)} %copy.26), kind=kLoop, calls=%fused_computation.3 | loop fusion | flops 6291456 | bytes 25165872 | tf_op jit(solution)/shard_map/jit(_take)/select_n | solution.py:30
  152.7 6.4 %gather_fusion.1 = bf16[48,64,2048]{2,1,0:T(8,128)(2,1)} fusion(bf16[8,64,2048]{2,1,0:T(8,128)(2,1)S(1)} %reshape.116, s32[1024]{0:T(1024)S(1)} %pad_clamp_fusion), kind=kCustom, calls=%fused_computation.1.clone | custom fusion | bytes 25166016 | tf_op jit(solution)/shard_map/jit(_take)/gather | solution.py:30
  159.0 12.5 %broadcast_select_fusion = bf16[24,2,64,2048]{3,2,1,0:T(8,128)(2,1)} fusion(bf16[24,2,64,2048]{3,2,1,0:T(8,128)(2,1)} %bitcast.69, pred[24,2]{1,0:T(8,128)(4,1)S(1)} %copy.35), kind=kLoop, calls=%fused_computation.2 | loop fusion | flops 6291456 | bytes 25165872 | tf_op jit(solution)/shard_map/jit(_take)/select_n | solution.py:30
  171.6 1.8 fusion
  173.4 11.0 %convolution_add_fusion = f32[24,64,2048]{2,1,0:T(8,128)} fusion(f32[24,64,2048]{2,1,0:T(8,128)S(1)} %fusion, bf16[24,128,2048]{2,1,0:T(8,128)(2,1)} %bitcast.66, bf16[24,1,2,64,128]{4,3,2,1,0:T(8,128)(2,1)S(1)} %copy-done.1, bf16[24,128]{1,0:T(8,128)(2,1)S(1)} %mul.35), kind=kOutput, calls=%fused_computation.4 | convolution fusion | flops 808648704 | bytes 38148096 | tf_op jit(solution)/shard_map/ixk,ikn->ixn/dot_general | solution.py:33
  184.4 134.6 %reduce-scatter.2.cloned.1.call-done = f32[96,2048]{1,0:T(8,128)} async-done(((f32[1536,2048]{1,0:T(8,128)}), f32[96,2048]{1,0:T(8,128)}) %reduce-scatter.2.cloned.1.call-update) | async-done | bytes 786448 | tf_op jit(solution)/shard_map/reduce_scatter | solution.py:73
  319.0 1.9 convert_element_type.37
  (10 shorter events, 0.0 us)
Async XLA Ops:
  6.5 35.8 %all-gather.3.cloned.1.call-start = ((), (), s32[]{:S(2)}) async-start(), calls=%async_computation.1 | async-start | bytes 3145728 | tf_op jit(solution)/shard_map/all_gather | solution.py:46
  7.3 95.8 %all-gather.5.cloned.1.call-start = ((), (), s32[]{:S(2)}) async-start(), calls=%async_computation.2 | async-start | bytes 10485760 | tf_op jit(solution)/shard_map/all_gather | solution.py:51
  42.3 276.7 %reduce-scatter.2.cloned.1.call-start = ((), (), s32[]{:S(2)}) async-start(), calls=%async_computation.3 | async-start | bytes 13369344 | tf_op jit(solution)/shard_map/reduce_scatter | solution.py:73
  159.0 12.5 %copy-start = (bf16[24,2,64,2048]{3,2,1,0:T(8,128)(2,1)S(1)}, bf16[24,2,64,2048]{3,2,1,0:T(8,128)(2,1)}, u32[]{:S(2)}) copy-start(bf16[24,2,64,2048]{3,2,1,0:T(8,128)(2,1)} %broadcast_select_fusion.1) | copy-start | bytes 37748740
  159.0 12.5 %copy-start.1 = (bf16[24,1,2,64,128]{4,3,2,1,0:T(8,128)(2,1)S(1)}, bf16[24,1,2,64,128]{4,3,2,1,0:T(8,128)(2,1)}, u32[]{:S(2)}) copy-start(bf16[24,1,2,64,128]{4,3,2,1,0:T(8,128)(2,1)} %param.9) | copy-start | bytes 2359300
Sparse Core Ops, SparseCore 0:
  8.9 33.3 all-gather.2
  43.9 59.1 all-gather.4
  184.5 134.4 reduce-scatter.1
where the time goes:
time: 331 us; the launch traced here: 327 us
  waiting for transfers between devices  202 us (61%)
  local copies, waits for them, and re-layouts  43.6 us (13%)
  other arithmetic  26.8 us (8%)
  blocking collectives  20.3 us (6%)
  matrix products  17.9 us (5%)
  between operations  17.2 us (5%)
    reduce_scatter x1, waiting for transfers between devices, body(): lax.psum_scatter(partial_terms, ('col', 'layer'), scatter_dimension=0, ti...  135 us
    all_gather x1, waiting for transfers between devices, body(): lax.all_gather(p_vals, 'row', axis=1, tiled=True)  35 us
    all_gather x1, waiting for transfers between devices, body(): lax.all_gather(section_vals, 'col', axis=3, tiled=True)  31.2 us
    select_n x3, other arithmetic, accumulate(): jnp.take(dense_rows, a_cols_panel, axis=0)  24 us
    gather x2, local copies, waits for them, and re-layouts, accumulate(): jnp.take(dense_rows, a_cols_panel, axis=0)  14.2 us
    dot_general x2, matrix products, accumulate(): jnp.einsum('ixk,ikn->ixn', masked, picked, preferred_element_type=jnp.flo...  12.8 us
    reshape x2, local copies, waits for them, and re-layouts, expand(): dense_rows.astype(jnp.bfloat16)  12.5 us
    all_gather x1, blocking collectives, body(): lax.all_gather(section_count, 'col', axis=3, tiled=True)  6.84 us
  transfers between devices with their start and end apart: 3, of which 3 were waited for; matrix products, arithmetic and copies ran while one was open for 2% of the time, Pallas kernels for 0%

commit v1 on v0

v1 whole, which is shorter than its diff:
```python
import functools

import jax
import jax.numpy as jnp
from jax import lax
from jax.experimental import pallas as pl
from jax.experimental.pallas import tpu as pltpu
from jax.sharding import PartitionSpec as P

CB = 8
MESH = pl.DeviceIdType.MESH


def swap_halves(tile):
    return pltpu.roll(tile.astype(jnp.float32), 64, 1).astype(jnp.bfloat16)


def masks_of(meta_row, lane_high):
    straight = (meta_row - lane_high).astype(jnp.float32)
    swapped = pltpu.roll(meta_row, 64, 1) - lane_high
    wide = lambda row: jnp.broadcast_to(row, (16, 128)).astype(jnp.bfloat16)
    return wide(straight), wide(swapped)


def kernel(
    sizes,
    pm_ref, a_ref, am_ref, p_ref, pq_ref, out_ref,
    ag, amg, pg, pqg, dense, lhs, part, up_in, down_in, fin, got,
    p_s, p_r, q_s, q_r, a_s, a_r, m_s, m_r, u_s, u_r, d_s, d_r, o_s, o_r,
):
    R, C, L = sizes
    row, col, layer = lax.axis_index("row"), lax.axis_index("col"), lax.axis_index("layer")
    panels_held, width_p = p_ref.shape[0], p_ref.shape[1]
    blocks, held = a_ref.shape[1], a_ref.shape[2]
    mate = col + 1 - 2 * lax.rem(col, 2)
    across = lax.rem(col + 2, 4)
    far = lax.rem(mate + 2, 4)
    owners = (col, mate, across, far)

    barrier = pltpu.get_barrier_semaphore()
    for j in range(1, R):
        pl.semaphore_signal(barrier, inc=1, device_id={"row": lax.rem(row + j, R)}, device_id_type=MESH)
    for j in range(1, C):
        pl.semaphore_signal(barrier, inc=1, device_id={"col": lax.rem(col + j, C)}, device_id_type=MESH)

    @pl.when(layer > 0)
    def _():
        pl.semaphore_signal(barrier, inc=1, device_id={"layer": layer - 1}, device_id_type=MESH)

    @pl.when(layer < L - 1)
    def _():
        pl.semaphore_signal(barrier, inc=1, device_id={"layer": layer + 1}, device_id_type=MESH)

    ends = (layer > 0).astype(jnp.int32) + (layer < L - 1).astype(jnp.int32)
    pl.semaphore_wait(barrier, R - 1 + C - 1 + ends)

    def remote(src, dst, send, recv, device):
        return pltpu.make_async_remote_copy(
            src_ref=src, dst_ref=dst, send_sem=send, recv_sem=recv, device_id=device, device_id_type=MESH
        )

    def p_copy(j, i, slot):
        return remote(p_ref.at[i], pg.at[slot, i], p_s.at[j, i], p_r.at[j, i], {"row": lax.rem(row + j, R)})

    def q_copy(j, slot):
        return remote(pq_ref, pqg.at[slot], q_s.at[j], q_r.at[j], {"row": lax.rem(row + j, R)})

    def a_copy(x, c):
        src = ag.at[1, c] if x == 3 else a_ref.at[c]
        return remote(src, ag.at[x - 1, c], a_s.at[x, c], a_r.at[x, c], {"col": across if x == 2 else mate})

    def m_copy(x):
        src = amg.at[1] if x == 3 else am_ref
        return remote(src, amg.at[x - 1], m_s.at[x], m_r.at[x], {"col": across if x == 2 else mate})

    for j in range(1, R):
        q_copy(j, row).start()
    m_copy(2).start()
    m_copy(1).start()
    for i in range(panels_held):
        for j in range(1, R):
            p_copy(j, i, row).start()
    for c in range(C):
        a_copy(2, c).start()
    for c in range(C):
        a_copy(1, c).start()

    lane_high = (lax.broadcasted_iota(jnp.int32, (1, 128), 1) >= 64).astype(jnp.float32)
    zero = jnp.zeros((4, 16, 128), jnp.bfloat16)

    def spread(tiles, keys, m):
        value = zero
        for tile, key in zip(tiles, keys):
            value = jnp.where((key == jnp.bfloat16(2 * m))[None], tile, value)
        return value.reshape(64, 128)

    def expand_panel(vals, meta, i, q):
        for w in range(width_p):
            tiles, keys = [], []
            for half in range(2):
                tile = vals[i, w, :, half * 128 : half * 128 + 128]
                tiles += [tile.reshape(4, 16, 128), swap_halves(tile).reshape(4, 16, 128)]
                keys += masks_of(meta[i, 2 * w + half : 2 * w + half + 1, :], lane_high)
            for m in range(CB // 2):
                dense[q, w * 64 : w * 64 + 64, m * 128 : m * 128 + 128] = spread(tiles, keys, m)

    @pl.loop(0, panels_held)
    def _(i):
        expand_panel(p_ref, pq_ref, i, row * panels_held + i)

    m_copy(2).wait_recv()
    m_copy(3).start()
    for c in range(C):
        a_copy(2, c).wait_recv()
        a_copy(3, c).start()

    for j in range(1, R):
        slot = lax.rem(row + R - j, R)
        q_copy(j, slot).wait_recv()

        @pl.loop(0, panels_held)
        def _(i):
            p_copy(j, i, slot).wait_recv()
            expand_panel(pg.at[slot], pqg.at[slot], i, slot * panels_held + i)

    m_copy(1).wait_recv()
    m_copy(3).wait_recv()

    def u_copy(d, c):
        return remote(part.at[c, d], up_in.at[c, d], u_s.at[c, d], u_r.at[c, d], {"layer": layer + 1})

    def d_copy(d, c):
        return remote(part.at[c, d], down_in.at[c, d], d_s.at[c, d], d_r.at[c, d], {"layer": layer - 1})

    rows_c = blocks * 64

    @pl.loop(0, C)
    def _(c):
        a_copy(1, c).wait_recv()
        a_copy(3, c).wait_recv()
        total = None
        for x in range(4):
            vals = a_ref if x == 0 else ag.at[x - 1]
            meta = am_ref if x == 0 else amg.at[x - 1]
            for k in range(held):
                slot = (x * held + k) % 2
                for b in range(blocks):
                    tile = vals[c, b, k]
                    tiles = [tile.reshape(4, 16, 128), swap_halves(tile).reshape(4, 16, 128)]
                    line = b * held + k
                    keys = masks_of(meta[c, line : line + 1, :], lane_high)
                    for m in range(CB // 2):
                        lhs[slot, b * 64 : b * 64 + 64, m * 128 : m * 128 + 128] = spread(tiles, keys, m)
                panel = pm_ref[layer, owners[x] * held + k]
                term = jnp.dot(lhs[slot], dense[panel], preferred_element_type=jnp.float32)
                total = term if total is None else total + term
        part[c] = total.reshape(part.shape[1:])

        @pl.when(layer == 0)
        def _():
            for d in range(L - 1, 0, -1):
                u_copy(d, c).start()

        @pl.when(layer == L - 1)
        def _():
            for d in range(L - 1):
                d_copy(d, c).start()

    def forward_up(c, d):
        @pl.when((layer > 0) & (layer < d))
        def _():
            u_copy(d, c).wait_recv()
            part[c, d] += up_in[c, d]
            u_copy(d, c).start()

    def forward_down(c, d):
        @pl.when((layer < L - 1) & (layer > d))
        def _():
            d_copy(d, c).wait_recv()
            part[c, d] += down_in[c, d]
            d_copy(d, c).start()

    def o_copy(c, slot):
        return remote(fin.at[c], got.at[slot], o_s.at[c], o_r.at[slot], {"col": c})

    @pl.loop(0, C)
    def _(c):
        for k in range(L - 1):
            @pl.when(layer >= L // 2)
            def _():
                forward_down(c, k)

            forward_up(c, L - 1 - k)

            @pl.when(layer < L // 2)
            def _():
                forward_down(c, k)

        @pl.when(layer > 0)
        def _():
            u_copy(layer, c).wait_recv()
            part[c, layer] += up_in[c, layer]

        @pl.when(layer < L - 1)
        def _():
            d_copy(layer, c).wait_recv()
            part[c, layer] += down_in[c, layer]

        result = part[c, layer].astype(jnp.bfloat16)

        @pl.when(col == c)
        def _():
            got[c] = result

        @pl.when(col != c)
        def _():
            fin[c] = result
            o_copy(c, col).start()

    for c in range(C):
        @pl.when(col != c)
        def _():
            o_copy(c, c).wait_recv()

        out_ref[:, c * CB * 64 : (c + 1) * CB * 64] = got[c]

    for j in range(1, R):
        q_copy(j, row).wait_send()
        for i in range(panels_held):
            p_copy(j, i, row).wait_send()
    for x in range(1, 4):
        m_copy(x).wait_send()
        for c in range(C):
            a_copy(x, c).wait_send()
    for c in range(C):
        for d in range(L):
            @pl.when(layer < d)
            def _():
                u_copy(d, c).wait_send()

            @pl.when(layer > d)
            def _():
                d_copy(d, c).wait_send()

        @pl.when(col != c)
        def _():
            o_copy(c, c).wait_send()


def lanes_of(cols, count):
    slots = cols.shape[-1]
    valid = jnp.arange(slots) < count[..., None]
    key = jnp.where(valid, cols, -64).astype(jnp.float32)
    wide = jnp.broadcast_to(key[..., None], key.shape + (64,))
    return wide.reshape(cols.shape[:-1] + (slots // 2, 128))


def body(sizes, a_vals, a_cols, a_count, panel_map, p_vals, p_cols, p_count):
    R, C, L = sizes
    rows_blk, _, held, side, wide = a_vals.shape
    blocks = rows_blk // C
    panels_held, width_p = p_vals.shape[1], p_vals.shape[2]
    a = a_vals.reshape(C, blocks, held, side, wide)
    lines = blocks * held
    am = lanes_of(a_cols[:, 0], a_count[:, 0]).reshape(C, lines, 128)
    pad = -lines % 8
    am = jnp.pad(am, ((0, 0), (0, pad), (0, 0)))
    p = p_vals.reshape(panels_held, width_p, side, p_vals.shape[-1])
    pq = lanes_of(p_cols[0, :, :, 0], p_count[0, :, :, 0]).reshape(panels_held, 2 * width_p, 128)
    piece = blocks * side // L
    width = CB * side
    f32, bf16 = jnp.float32, jnp.bfloat16
    sems = pltpu.SemaphoreType.DMA
    vmem = pl.BlockSpec(memory_space=pltpu.VMEM)
    return pl.pallas_call(
        functools.partial(kernel, sizes),
        out_shape=jax.ShapeDtypeStruct((piece, C * width), bf16),
        in_specs=[pl.BlockSpec(memory_space=pltpu.SMEM), vmem, vmem, vmem, vmem],
        out_specs=vmem,
        scratch_shapes=[
            pltpu.VMEM((3,) + a.shape, bf16),
            pltpu.VMEM((3,) + am.shape, f32),
            pltpu.VMEM((R,) + p.shape, bf16),
            pltpu.VMEM((R,) + pq.shape, f32),
            pltpu.VMEM((R * panels_held, width_p * side, width), bf16),
            pltpu.VMEM((2, blocks * side, width_p * side), bf16),
            pltpu.VMEM((C, L, piece, width), f32),
            pltpu.VMEM((C, L, piece, width), f32),
            pltpu.VMEM((C, L, piece, width), f32),
            pltpu.VMEM((C, piece, width), bf16),
            pltpu.VMEM((C, piece, width), bf16),
            sems((R, panels_held)), sems((R, panels_held)), sems((R,)), sems((R,)),
            sems((4, C)), sems((4, C)), sems((4,)), sems((4,)),
            sems((C, L)), sems((C, L)), sems((C, L)), sems((C, L)),
            sems((C,)), sems((C,)),
        ],
        compiler_params=pltpu.CompilerParams(
            collective_id=0, has_side_effects=True, vmem_limit_bytes=56 * 1024 * 1024
        ),
        cost_estimate=pl.CostEstimate(flops=7 * 10**9, bytes_accessed=3 * 10**6, transcendentals=0),
    )(panel_map, a, am, p, pq)


def solution(mesh):
    placed = (
        P("row", "layer", "col", None, None),
        P("row", "layer", "col", None),
        P("row", "layer", "col"),
        P(),
        P("layer", "row", None, "col", None, None),
        P("layer", "row", None, "col", None),
        P("layer", "row", None, "col"),
    )
    sizes = (mesh.shape["row"], mesh.shape["col"], mesh.shape["layer"])
    return jax.shard_map(
        functools.partial(body, sizes),
        mesh=mesh,
        in_specs=placed,
        out_specs=P(("row", "col", "layer"), None),
        check_vma=False,
    )
```

time: 331 us -> 97.5 us (0.29)
  waiting for transfers between devices: 202 us -> 0 us
  Pallas kernels: 0 us -> 91.5 us
  local copies, waits for them, and re-layouts: 43.6 us -> 3.59 us
  other arithmetic: 26.8 us -> 0.73 us
  blocking collectives: 20.3 us -> 0 us
  matrix products: 17.9 us -> 0 us
  between operations: 17.2 us -> 0.04 us
    reduce_scatter x1 -> x0, waiting for transfers between devices: 135 us -> none  [body(): lax.psum_scatter(partial_terms, ('col', 'layer'), scatter_dimension=0, ti...]
    pallas_call x0 -> x1, Pallas kernels: none -> 91.5 us  [body(): pl.pallas_call(functools.partial(kernel, sizes), out_shape=jax.ShapeDtype...]
    all_gather x2 -> x0, waiting for transfers between devices: 66.2 us -> none  [the longest x1 35 us: body(): lax.all_gather(p_vals, 'row', axis=1, tiled=True)]
    select_n x3 -> x0, other arithmetic: 24 us -> none  [accumulate(): jnp.take(dense_rows, a_cols_panel, axis=0)]
    all_gather x4 -> x0, blocking collectives: 20.3 us -> none  [the longest x1 6.84 us: body(): lax.all_gather(section_count, 'col', axis=3, tiled=True)]
    dot_general x4 -> x0, matrix products: 17.9 us -> none  [the longest x2 12.8 us: accumulate(): jnp.einsum('ixk,ikn->ixn', masked, picked, preferred_element_type=jnp.flo...]
    reshape x4 -> x0, local copies, waits for them, and re-layouts: 17.7 us -> none  [the longest x2 12.5 us: expand(): dense_rows.astype(jnp.bfloat16)]
    gather x2 -> x0, local copies, waits for them, and re-layouts: 14.2 us -> none  [accumulate(): jnp.take(dense_rows, a_cols_panel, axis=0)]
  transfers between devices with their start and end apart: 3 -> 0, of which waited for: 3 -> 0; matrix products, arithmetic and copies ran while one was open for 2% -> 0% of each run, Pallas kernels for 0% -> 0%
where the time goes in v1:
time: 97.5 us; the launch traced here: 95.9 us
  Pallas kernels  91.5 us (94%)
  local copies, waits for them, and re-layouts  3.59 us (4%)
    pallas_call x1, Pallas kernels, body(): pl.pallas_call(functools.partial(kernel, sizes), out_shape=jax.ShapeDtype...  91.5 us

profile of v1, /device:TPU:7, one launch (start us, length us, event | category | flops | bytes accessed | tf_op | source)
XLA Modules:
  0.0 95.9 jit_solution(18024071230558332660)
XLA Ops:
  0.0 0.0 copy-start
  0.0 0.0 copy-start.1
  0.0 0.7 fusion.1
  0.7 0.0 copy-done
  0.7 0.0 copy-done.1
  0.8 0.1 copy.11
  0.9 0.1 copy.10
  1.0 0.1 broadcast_in_dim.13
  1.1 0.1 reshape_reshape.6
  1.2 0.6 pad.4.am_ref
  1.8 0.1 broadcast_in_dim.25
  1.9 0.7 reshape_reshape.7.pq_ref
  2.6 91.5 %shard_map.73 = bf16[96,2048]{1,0:T(8,128)(2,1)} custom-call(s32[4,8]{1,0:T(4,128)} %pm_ref.1, bf16[4,6,2,64,128]{4,3,2,1,0:T(8,128)(2,1)} %bitcast.13, f32[4,16,128]{2,1,0:T(8,128)} %pad.4.am_ref, bf16[4,8,64,256]{3,2,1,0:T(8,128)(2,1)} %bitcast.12, f32[4,16,128]{2,1,0:T(8,128)} %reshape_reshape.7.pq_ref), custom_call_target="tpu_custom_call" | custom-call | flops 7000000000 | bytes 3000000 | tf_op jit(solution)/shard_map/pallas_call | solution.py:275
  94.1 1.8 %copy.13 = bf16[96,2048]{1,0:T(8,128)(2,1)} copy(bf16[96,2048]{1,0:T(8,128)(2,1)} %shard_map.73) | data formatting | bytes 786432
  (1 shorter events, 0.0 us)
Async XLA Ops:
  0.0 0.7 copy-start
  0.0 0.7 copy-start.1

commit v2 on v1

--- a/solution.py
+++ b/solution.py
@@ -22,11 +22,37 @@
     return wide(straight), wide(swapped)
 
 
+FULL = float(2**22)
+
+
+def encode(value):
+    rows, width = value.shape
+    grouped = value.reshape(rows // 8, 8, width)
+    most = jnp.max(jnp.abs(grouped), axis=0)
+    most = functools.reduce(jnp.maximum, [most[:, i : i + 128] for i in range(0, width, 128)])
+    most = jnp.maximum(most, 1e-31)
+    factor = jnp.concatenate([FULL / most] * (width // 128), axis=1)
+    fixed = jnp.round(grouped * factor[None]).astype(jnp.int32).reshape(rows, width)
+    high = lax.shift_right_arithmetic(fixed, 8).astype(jnp.int16)
+    low = fixed & 255
+    low = (low[:, : width // 2] * 256 + low[:, width // 2 :] - 32768).astype(jnp.int16)
+    return high, low, most * (1.0 / FULL)
+
+
+def decode(high, low, scale):
+    rows, width = high.shape
+    pair = low.astype(jnp.int32) + 32768
+    low = jnp.concatenate([lax.shift_right_arithmetic(pair, 8), pair & 255], axis=1)
+    fixed = (high.astype(jnp.int32) * 256 + low).astype(jnp.float32)
+    factor = jnp.concatenate([scale] * (width // 128), axis=1)
+    return (fixed.reshape(rows // 8, 8, width) * factor[None]).reshape(rows, width)
+
+
 def kernel(
     sizes,
     pm_ref, a_ref, am_ref, p_ref, pq_ref, out_ref,
-    ag, amg, pg, pqg, dense, lhs, part, up_in, down_in, fin, got,
-    p_s, p_r, q_s, q_r, a_s, a_r, m_s, m_r, u_s, u_r, d_s, d_r, o_s, o_r,
+    ag, amg, pg, pqg, dense, lhs, part, tx, txs, up_in, up_sc, down_in, down_sc, fin, got,
+    p_s, p_r, q_s, q_r, a_s, a_r, m_s, m_r, u_s, u_r, us_s, us_r, d_s, d_r, ds_s, ds_r, o_s, o_r,
 ):
     R, C, L = sizes
     row, col, layer = lax.axis_index("row"), lax.axis_index("col"), lax.axis_index("layer")
@@ -126,13 +152,34 @@
     m_copy(1).wait_recv()
     m_copy(3).wait_recv()
 
-    def u_copy(d, c):
-        return remote(part.at[c, d], up_in.at[c, d], u_s.at[c, d], u_r.at[c, d], {"layer": layer + 1})
-
-    def d_copy(d, c):
-        return remote(part.at[c, d], down_in.at[c, d], d_s.at[c, d], d_r.at[c, d], {"layer": layer - 1})
-
-    rows_c = blocks * 64
+    wide_out = part.shape[3]
+
+    def u_copies(d, c):
+        to = {"layer": layer + 1}
+        return (
+            remote(txs.at[c, d], up_sc.at[c, d], us_s.at[c, d], us_r.at[c, d], to),
+            remote(tx.at[c, d], up_in.at[c, d], u_s.at[c, d], u_r.at[c, d], to),
+        )
+
+    def d_copies(d, c):
+        to = {"layer": layer - 1}
+        return (
+            remote(txs.at[c, d], down_sc.at[c, d], ds_s.at[c, d], ds_r.at[c, d], to),
+            remote(tx.at[c, d], down_in.at[c, d], d_s.at[c, d], d_r.at[c, d], to),
+        )
+
+    def send(copies, d, c, value):
+        high, low, scale = encode(value)
+        tx[c, d, :, :wide_out] = high
+        tx[c, d, :, wide_out:] = low
+        txs[c, d] = scale
+        for copy in copies(d, c):
+            copy.start()
+
+    def received(copies, ref, scales, d, c):
+        for copy in copies(d, c):
+            copy.wait_recv()
+        return decode(ref[c, d, :, :wide_out], ref[c, d, :, wide_out:], scales[c, d])
 
     @pl.loop(0, C)
     def _(c):
@@ -159,26 +206,22 @@
         @pl.when(layer == 0)
         def _():
             for d in range(L - 1, 0, -1):
-                u_copy(d, c).start()
+                send(u_copies, d, c, part[c, d])
 
         @pl.when(layer == L - 1)
         def _():
             for d in range(L - 1):
-                d_copy(d, c).start()
+                send(d_copies, d, c, part[c, d])
 
     def forward_up(c, d):
         @pl.when((layer > 0) & (layer < d))
         def _():
-            u_copy(d, c).wait_recv()
-            part[c, d] += up_in[c, d]
-            u_copy(d, c).start()
+            send(u_copies, d, c, part[c, d] + received(u_copies, up_in, up_sc, d, c))
 
     def forward_down(c, d):
         @pl.when((layer < L - 1) & (layer > d))
         def _():
-            d_copy(d, c).wait_recv()
-            part[c, d] += down_in[c, d]
-            d_copy(d, c).start()
+            send(d_copies, d, c, part[c, d] + received(d_copies, down_in, down_sc, d, c))
 
     def o_copy(c, slot):
         return remote(fin.at[c], got.at[slot], o_s.at[c], o_r.at[slot], {"col": c})
@@ -198,13 +241,11 @@
 
         @pl.when(layer > 0)
         def _():
-            u_copy(layer, c).wait_recv()
-            part[c, layer] += up_in[c, layer]
+            part[c, layer] += received(u_copies, up_in, up_sc, layer, c)
 
         @pl.when(layer < L - 1)
         def _():
-            d_copy(layer, c).wait_recv()
-            part[c, layer] += down_in[c, layer]
+            part[c, layer] += received(d_copies, down_in, down_sc, layer, c)
 
         result = part[c, layer].astype(jnp.bfloat16)
 
@@ -236,11 +277,13 @@
         for d in range(L):
             @pl.when(layer < d)
             def _():
-                u_copy(d, c).wait_send()
+                for copy in u_copies(d, c):
+                    copy.wait_send()
 
             @pl.when(layer > d)
             def _():
-                d_copy(d, c).wait_send()
+                for copy in d_copies(d, c):
+                    copy.wait_send()
 
         @pl.when(col != c)
         def _():
@@ -271,6 +314,8 @@
     width = CB * side
     f32, bf16 = jnp.float32, jnp.bfloat16
     sems = pltpu.SemaphoreType.DMA
+    coded = pltpu.VMEM((C, L, piece, width + width // 2), jnp.int16)
+    scales = pltpu.VMEM((C, L, 8, 128), f32)
     vmem = pl.BlockSpec(memory_space=pltpu.VMEM)
     return pl.pallas_call(
         functools.partial(kernel, sizes),
@@ -285,13 +330,12 @@
             pltpu.VMEM((R * panels_held, width_p * side, width), bf16),
             pltpu.VMEM((2, blocks * side, width_p * side), bf16),
             pltpu.VMEM((C, L, piece, width), f32),
-            pltpu.VMEM((C, L, piece, width), f32),
-            pltpu.VMEM((C, L, piece, width), f32),
+            *[coded, scales] * 3,
             pltpu.VMEM((C, piece, width), bf16),
             pltpu.VMEM((C, piece, width), bf16),
             sems((R, panels_held)), sems((R, panels_held)), sems((R,)), sems((R,)),
             sems((4, C)), sems((4, C)), sems((4,)), sems((4,)),
-            sems((C, L)), sems((C, L)), sems((C, L)), sems((C, L)),
+            *[sems((C, L))] * 8,
             sems((C,)), sems((C,)),
         ],
         compiler_params=pltpu.CompilerParams(

time: 97.5 us -> 89.5 us (0.918)
  Pallas kernels: 91.5 us -> 83.5 us
    pallas_call x1, Pallas kernels: 91.5 us -> 83.5 us  [body(): pl.pallas_call(functools.partial(kernel, sizes), out_shape=jax.ShapeDtype...]
where the time goes in v2:
time: 89.5 us; the launch traced here: 87.8 us
  Pallas kernels  83.5 us (93%)
  local copies, waits for them, and re-layouts  3.59 us (4%)
    pallas_call x1, Pallas kernels, body(): pl.pallas_call(functools.partial(kernel, sizes), out_shape=jax.ShapeDtype...  83.5 us

profile of v2, /device:TPU:7, one launch (start us, length us, event | category | flops | bytes accessed | tf_op | source)
XLA Modules:
  0.0 87.8 jit_solution(16376773346223371042)
XLA Ops:
  0.0 0.0 copy-start
  0.0 0.0 copy-start.1
  0.0 0.7 fusion.1
  0.7 0.0 copy-done
  0.7 0.0 copy-done.1
  0.8 0.1 copy.11
  0.9 0.1 copy.10
  1.0 0.1 broadcast_in_dim.13
  1.1 0.1 reshape_reshape.6
  1.2 0.6 pad.4.am_ref
  1.8 0.1 broadcast_in_dim.25
  1.9 0.7 reshape_reshape.7.pq_ref
  2.6 83.5 %shard_map.73 = bf16[96,2048]{1,0:T(8,128)(2,1)} custom-call(s32[4,8]{1,0:T(4,128)} %pm_ref.1, bf16[4,6,2,64,128]{4,3,2,1,0:T(8,128)(2,1)} %bitcast.13, f32[4,16,128]{2,1,0:T(8,128)} %pad.4.am_ref, bf16[4,8,64,256]{3,2,1,0:T(8,128)(2,1)} %bitcast.12, f32[4,16,128]{2,1,0:T(8,128)} %reshape_reshape.7.pq_ref), custom_call_target="tpu_custom_call" | custom-call | flops 7000000000 | bytes 3000000 | tf_op jit(solution)/shard_map/pallas_call | solution.py:320
  86.1 1.8 %copy.13 = bf16[96,2048]{1,0:T(8,128)(2,1)} copy(bf16[96,2048]{1,0:T(8,128)(2,1)} %shard_map.73) | data formatting | bytes 786432
  (1 shorter events, 0.0 us)
Async XLA Ops:
  0.0 0.7 copy-start
  0.0 0.7 copy-start.1

commit v3 on v2

--- a/solution.py
+++ b/solution.py
@@ -50,7 +50,7 @@
 
 def kernel(
     sizes,
-    pm_ref, a_ref, am_ref, p_ref, pq_ref, out_ref,
+    slot_ref, a_ref, am_ref, p_ref, pq_ref, out_ref,
     ag, amg, pg, pqg, dense, lhs, part, tx, txs, up_in, up_sc, down_in, down_sc, fin, got,
     p_s, p_r, q_s, q_r, a_s, a_r, m_s, m_r, u_s, u_r, us_s, us_r, d_s, d_r, ds_s, ds_r, o_s, o_r,
 ):
@@ -60,8 +60,6 @@
     blocks, held = a_ref.shape[1], a_ref.shape[2]
     mate = col + 1 - 2 * lax.rem(col, 2)
     across = lax.rem(col + 2, 4)
-    far = lax.rem(mate + 2, 4)
-    owners = (col, mate, across, far)
 
     barrier = pltpu.get_barrier_semaphore()
     for j in range(1, R):
@@ -130,27 +128,76 @@
             for m in range(CB // 2):
                 dense[q, w * 64 : w * 64 + 64, m * 128 : m * 128 + 128] = spread(tiles, keys, m)
 
+    def expand_chunk(x, c):
+        vals = a_ref if x == 0 else ag.at[x - 1]
+        meta = am_ref if x == 0 else amg.at[x - 1]
+        for k in range(held):
+            for b in range(blocks):
+                tile = vals[c, b, k]
+                tiles = [tile.reshape(4, 16, 128), swap_halves(tile).reshape(4, 16, 128)]
+                line = b * held + k
+                keys = masks_of(meta[c, line : line + 1, :], lane_high)
+                for m in range(CB // 2):
+                    lhs[x * held + k, c, b * 64 : b * 64 + 64, m * 128 : m * 128 + 128] = spread(tiles, keys, m)
+
+    def product(c, q):
+        term = jnp.dot(lhs[slot_ref[q], c], dense[q], preferred_element_type=jnp.float32)
+        return term.reshape(part.shape[1:])
+
+    def add(c, q):
+        part[c] += product(c, q)
+
+    def take_panel(n):
+        j, i = 1 + n // panels_held, n % panels_held
+        slot = lax.rem(row + R - j, R)
+        if i == 0:
+            q_copy(j, slot).wait_recv()
+        p_copy(j, i, slot).wait_recv()
+        expand_panel(pg.at[slot], pqg.at[slot], i, slot * panels_held + i)
+        return slot * panels_held + i
+
     @pl.loop(0, panels_held)
     def _(i):
         expand_panel(p_ref, pq_ref, i, row * panels_held + i)
 
+    @pl.loop(0, C)
+    def _(c):
+        part[c] = jnp.zeros(part.shape[1:], jnp.float32)
+        expand_chunk(0, c)
+
+    m_copy(1).wait_recv()
     m_copy(2).wait_recv()
     m_copy(3).start()
+    others = (R - 1) * panels_held
+    each = -(-(others - 1) // (C - 1))
+    taken = []
     for c in range(C):
         a_copy(2, c).wait_recv()
         a_copy(3, c).start()
-
-    for j in range(1, R):
-        slot = lax.rem(row + R - j, R)
-        q_copy(j, slot).wait_recv()
+        a_copy(1, c).wait_recv()
+        expand_chunk(1, c)
+        expand_chunk(2, c)
+        if c == 0:
+            m_copy(3).wait_recv()
+        a_copy(3, c).wait_recv()
+        expand_chunk(3, c)
 
         @pl.loop(0, panels_held)
         def _(i):
-            p_copy(j, i, slot).wait_recv()
-            expand_panel(pg.at[slot], pqg.at[slot], i, slot * panels_held + i)
-
-    m_copy(1).wait_recv()
-    m_copy(3).wait_recv()
+            add(c, row * panels_held + i)
+
+        for q in taken:
+            add(c, q)
+        if c:
+            for n in range((c - 1) * each, min(c * each, others - 1)):
+                q = take_panel(n)
+                taken.append(q)
+
+                @pl.loop(0, c + 1)
+                def _(earlier):
+                    add(earlier, q)
+
+    last = take_panel(others - 1)
 
     wide_out = part.shape[3]
 
@@ -183,25 +230,7 @@
 
     @pl.loop(0, C)
     def _(c):
-        a_copy(1, c).wait_recv()
-        a_copy(3, c).wait_recv()
-        total = None
-        for x in range(4):
-            vals = a_ref if x == 0 else ag.at[x - 1]
-            meta = am_ref if x == 0 else amg.at[x - 1]
-            for k in range(held):
-                slot = (x * held + k) % 2
-                for b in range(blocks):
-                    tile = vals[c, b, k]
-                    tiles = [tile.reshape(4, 16, 128), swap_halves(tile).reshape(4, 16, 128)]
-                    line = b * held + k
-                    keys = masks_of(meta[c, line : line + 1, :], lane_high)
-                    for m in range(CB // 2):
-                        lhs[slot, b * 64 : b * 64 + 64, m * 128 : m * 128 + 128] = spread(tiles, keys, m)
-                panel = pm_ref[layer, owners[x] * held + k]
-                term = jnp.dot(lhs[slot], dense[panel], preferred_element_type=jnp.float32)
-                total = term if total is None else total + term
-        part[c] = total.reshape(part.shape[1:])
+        add(c, last)
 
         @pl.when(layer == 0)
         def _():
@@ -310,6 +339,15 @@
     am = jnp.pad(am, ((0, 0), (0, pad), (0, 0)))
     p = p_vals.reshape(panels_held, width_p, side, p_vals.shape[-1])
     pq = lanes_of(p_cols[0, :, :, 0], p_count[0, :, :, 0]).reshape(panels_held, 2 * width_p, 128)
+    col = lax.axis_index("col")
+    layer_map = lax.dynamic_index_in_dim(panel_map, lax.axis_index("layer"), 0, keepdims=False)
+    sections = jnp.arange(layer_map.shape[0], dtype=jnp.int32)
+    owner = sections // held
+    mate = col + 1 - 2 * (col % 2)
+    across = (col + 2) % 4
+    place = jnp.where(owner == col, 0, jnp.where(owner == mate, 1, jnp.where(owner == across, 2, 3)))
+    place = (place * held + sections % held).astype(jnp.int32)
+    slots = jnp.sum(jnp.where(layer_map[None, :] == sections[:, None], place[None, :], 0), axis=1)
     piece = blocks * side // L
     width = CB * side
     f32, bf16 = jnp.float32, jnp.bfloat16
@@ -328,7 +366,7 @@
             pltpu.VMEM((R,) + p.shape, bf16),
             pltpu.VMEM((R,) + pq.shape, f32),
             pltpu.VMEM((R * panels_held, width_p * side, width), bf16),
-            pltpu.VMEM((2, blocks * side, width_p * side), bf16),
+            pltpu.VMEM((C * held, C, blocks * side, width_p * side), bf16),
             pltpu.VMEM((C, L, piece, width), f32),
             *[coded, scales] * 3,
             pltpu.VMEM((C, piece, width), bf16),
@@ -342,7 +380,7 @@
             collective_id=0, has_side_effects=True, vmem_limit_bytes=56 * 1024 * 1024
         ),
         cost_estimate=pl.CostEstimate(flops=7 * 10**9, bytes_accessed=3 * 10**6, transcendentals=0),
-    )(panel_map, a, am, p, pq)
+    )(slots, a, am, p, pq)
 
 
 def solution(mesh):

time: 89.5 us -> 89.1 us (level)
  Pallas kernels: 83.5 us -> 80.9 us
  local copies, waits for them, and re-layouts: 3.59 us -> 5.63 us
    pallas_call x1, Pallas kernels: 83.5 us -> 80.9 us  [body(): pl.pallas_call(functools.partial(kernel, sizes), out_shape=jax.ShapeDtype...]
    unnamed x5 -> x11, local copies, waits for them, and re-layouts: 1.77 us -> 3.8 us
where the time goes in v3:
time: 89.1 us; the launch traced here: 87.3 us
  Pallas kernels  80.9 us (91%)
  local copies, waits for them, and re-layouts  5.63 us (6%)
    pallas_call x1, Pallas kernels, body(): pl.pallas_call(functools.partial(kernel, sizes), out_shape=jax.ShapeDtype...  80.9 us
    unnamed x11, local copies, waits for them, and re-layouts  3.8 us

profile of v3, /device:TPU:7, one launch (start us, length us, event | category | flops | bytes accessed | tf_op | source)
XLA Modules:
  0.0 87.3 jit_solution(1625535264838114393)
XLA Ops:
  0.0 0.0 copy-start
  0.0 0.0 copy-start.1
  0.0 0.7 copy-done
  0.7 0.7 select_reduce_fusion.slot_ref
  1.4 0.0 copy-start.3
  1.4 0.0 copy-start.4
  1.4 0.7 copy-done.3
  2.1 0.0 copy-done.4
  2.1 0.0 copy-start.2
  2.1 0.0 copy-done.1
  2.1 0.7 copy-done.2
  2.8 0.1 copy.13
  2.9 0.1 copy.12
  3.0 0.1 broadcast_in_dim.50
  3.1 0.1 reshape_reshape.6
  3.2 0.6 pad.4.am_ref
  3.8 0.1 broadcast_in_dim.52
  3.9 0.7 reshape_reshape.7.pq_ref
  4.6 80.9 %shard_map.73 = bf16[96,2048]{1,0:T(8,128)(2,1)} custom-call(s32[8]{0:T(128)} %select_reduce_fusion.slot_ref, bf16[4,6,2,64,128]{4,3,2,1,0:T(8,128)(2,1)} %bitcast.15, f32[4,16,128]{2,1,0:T(8,128)} %pad.4.am_ref, bf16[4,8,64,256]{3,2,1,0:T(8,128)(2,1)} %bitcast.14, f32[4,16,128]{2,1,0:T(8,128)} %reshape_reshape.7.pq_ref), custom_call_target="tpu_custom_call" | custom-call | flops 7000000000 | bytes 3000000 | tf_op jit(solution)/shard_map/pallas_call | solution.py:358
  85.6 1.8 %copy.15 = bf16[96,2048]{1,0:T(8,128)(2,1)} copy(bf16[96,2048]{1,0:T(8,128)(2,1)} %shard_map.73) | data formatting | bytes 786432
  (4 shorter events, 0.0 us)
Async XLA Ops:
  0.0 0.7 copy-start
  0.0 2.1 %copy-start.1 = (s32[1,4,8,1,4]{2,4,3,1,0:T(4,128)S(1)}, s32[1,4,8,1,4]{2,4,3,1,0:T(4,128)}, u32[]{:S(2)}) copy-start(s32[1,4,8,1,4]{2,4,3,1,0:T(4,128)} %param.12) | copy-start | bytes 1540
  1.4 0.7 copy-start.3
  1.4 0.7 copy-start.4
  2.1 0.7 copy-start.2

commit v4 on v3

--- a/solution.py
+++ b/solution.py
@@ -101,13 +101,22 @@
         q_copy(j, row).start()
     m_copy(2).start()
     m_copy(1).start()
-    for i in range(panels_held):
-        for j in range(1, R):
-            p_copy(j, i, row).start()
-    for c in range(C):
+    others = (R - 1) * panels_held
+
+    def p_nth(n):
+        return p_copy(1 + n // panels_held, n % panels_held, row)
+
+    for n in range(min(2, others)):
+        p_nth(n).start()
+    for c in range(2):
         a_copy(2, c).start()
     for c in range(C):
         a_copy(1, c).start()
+
+    def next_p(n):
+        if n + 2 < others:
+            p_nth(n).wait_send()
+            p_nth(n + 2).start()
 
     lane_high = (lax.broadcasted_iota(jnp.int32, (1, 128), 1) >= 64).astype(jnp.float32)
     zero = jnp.zeros((4, 16, 128), jnp.bfloat16)
@@ -168,12 +177,16 @@
     m_copy(1).wait_recv()
     m_copy(2).wait_recv()
     m_copy(3).start()
-    others = (R - 1) * panels_held
     each = -(-(others - 1) // (C - 1))
     taken = []
     for c in range(C):
         a_copy(2, c).wait_recv()
         a_copy(3, c).start()
+        if c + 2 < C:
+            a_copy(2, c).wait_send()
+            a_copy(2, c + 2).start()
+        for n in range(c, others) if c == C - 1 else (c,):
+            next_p(n)
         a_copy(1, c).wait_recv()
         expand_chunk(1, c)
         expand_chunk(2, c)
@@ -215,11 +228,17 @@
             remote(tx.at[c, d], down_in.at[c, d], d_s.at[c, d], d_r.at[c, d], to),
         )
 
-    def send(copies, d, c, value):
+    def stage(d, c, value):
         high, low, scale = encode(value)
         tx[c, d, :, :wide_out] = high
         tx[c, d, :, wide_out:] = low
         txs[c, d] = scale
+
+    def send(copies, d, c, value):
+        stage(d, c, value)
+        launch(copies, d, c)
+
+    def launch(copies, d, c):
         for copy in copies(d, c):
             copy.start()
 
@@ -228,19 +247,33 @@
             copy.wait_recv()
         return decode(ref[c, d, :, :wide_out], ref[c, d, :, wide_out:], scales[c, d])
 
+    def send_all(copies, order, c):
+        order = list(order)
+        for n, d in enumerate(order):
+            stage(d, c, part[c, d])
+            if n >= 2:
+                sent(copies, order[n - 2], c)
+            else:
+                @pl.when(c > 0)
+                def _():
+                    sent(copies, order[len(order) - 2 + n], c - 1)
+            launch(copies, d, c)
+
+    def sent(copies, d, c):
+        for copy in copies(d, c):
+            copy.wait_send()
+
     @pl.loop(0, C)
     def _(c):
         add(c, last)
 
         @pl.when(layer == 0)
         def _():
-            for d in range(L - 1, 0, -1):
-                send(u_copies, d, c, part[c, d])
+            send_all(u_copies, range(L - 1, 0, -1), c)
 
         @pl.when(layer == L - 1)
         def _():
-            for d in range(L - 1):
-                send(d_copies, d, c, part[c, d])
+            send_all(d_copies, range(L - 1), c)
 
     def forward_up(c, d):
         @pl.when((layer > 0) & (layer < d))
@@ -296,23 +329,21 @@
 
     for j in range(1, R):
         q_copy(j, row).wait_send()
-        for i in range(panels_held):
-            p_copy(j, i, row).wait_send()
+    for n in range(max(others - 2, 0), others):
+        p_nth(n).wait_send()
     for x in range(1, 4):
         m_copy(x).wait_send()
-        for c in range(C):
+        for c in range(C - 2 if x == 2 else 0, C):
             a_copy(x, c).wait_send()
     for c in range(C):
         for d in range(L):
-            @pl.when(layer < d)
+            @pl.when((layer < d) & ((layer > 0) | ((c == C - 1) & (d <= 2))))
             def _():
-                for copy in u_copies(d, c):
-                    copy.wait_send()
-
-            @pl.when(layer > d)
+                sent(u_copies, d, c)
+
+            @pl.when((layer > d) & ((layer < L - 1) | ((c == C - 1) & (d >= L - 3))))
             def _():
-                for copy in d_copies(d, c):
-                    copy.wait_send()
+                sent(d_copies, d, c)
 
         @pl.when(col != c)
         def _():

time: 89.1 us -> 94 us (1.055); the launches traced: 87.3 us -> 93.7 us
  Pallas kernels: 80.9 us -> 87.3 us
    pallas_call x1, Pallas kernels: 80.9 us -> 87.3 us  [body(): pl.pallas_call(functools.partial(kernel, sizes), out_shape=jax.ShapeDtype...]
where the time goes in v4:
time: 94 us; the launch traced here: 93.7 us
  Pallas kernels  87.3 us (93%)
  local copies, waits for them, and re-layouts  5.63 us (6%)
    pallas_call x1, Pallas kernels, body(): pl.pallas_call(functools.partial(kernel, sizes), out_shape=jax.ShapeDtype...  87.3 us
    unnamed x11, local copies, waits for them, and re-layouts  3.8 us

profile of v4, /device:TPU:7, one launch (start us, length us, event | category | flops | bytes accessed | tf_op | source)
XLA Modules:
  0.0 93.7 jit_solution(16557635490112422908)
XLA Ops:
  0.0 0.0 copy-start
  0.0 0.0 copy-start.1
  0.0 0.7 copy-done
  0.7 0.7 select_reduce_fusion.slot_ref
  1.4 0.0 copy-start.3
  1.4 0.0 copy-start.4
  1.4 0.7 copy-done.3
  2.1 0.0 copy-done.4
  2.1 0.0 copy-start.2
  2.1 0.0 copy-done.1
  2.1 0.7 copy-done.2
  2.8 0.1 copy.13
  2.9 0.1 copy.12
  3.0 0.1 broadcast_in_dim.50
  3.1 0.1 reshape_reshape.6
  3.2 0.6 pad.4.am_ref
  3.8 0.1 broadcast_in_dim.52
  3.9 0.7 reshape_reshape.7.pq_ref
  4.6 87.3 %shard_map.73 = bf16[96,2048]{1,0:T(8,128)(2,1)} custom-call(s32[8]{0:T(128)} %select_reduce_fusion.slot_ref, bf16[4,6,2,64,128]{4,3,2,1,0:T(8,128)(2,1)} %bitcast.15, f32[4,16,128]{2,1,0:T(8,128)} %pad.4.am_ref, bf16[4,8,64,256]{3,2,1,0:T(8,128)(2,1)} %bitcast.14, f32[4,16,128]{2,1,0:T(8,128)} %reshape_reshape.7.pq_ref), custom_call_target="tpu_custom_call" | custom-call | flops 7000000000 | bytes 3000000 | tf_op jit(solution)/shard_map/pallas_call | solution.py:389
  91.9 1.8 %copy.15 = bf16[96,2048]{1,0:T(8,128)(2,1)} copy(bf16[96,2048]{1,0:T(8,128)(2,1)} %shard_map.73) | data formatting | bytes 786432
  (4 shorter events, 0.0 us)
Async XLA Ops:
  0.0 0.7 copy-start
  0.0 2.1 %copy-start.1 = (s32[1,4,8,1,4]{2,4,3,1,0:T(4,128)S(1)}, s32[1,4,8,1,4]{2,4,3,1,0:T(4,128)}, u32[]{:S(2)}) copy-start(s32[1,4,8,1,4]{2,4,3,1,0:T(4,128)} %param.12) | copy-start | bytes 1540
  1.4 0.7 copy-start.3
  1.4 0.7 copy-start.4
  2.1 0.7 copy-start.2
